TPU v7x, 128 devices: a whole 4x4x4 slice. The times are simulated.
128 devices in a mesh: row: 16 (over x_lo, z, core), col: 8 (over x_hi, y).
Axes of the slice: x: 4 (x_hi: 2, x_lo: 2; x = x_hi * 2 + x_lo), y: 4, z: 4, core: 2. Of those that a mesh axis runs over, the one named last changes fastest.
Arguments:
- tile_values: bfloat16 [16, 8, 384, 128, 128], P('row', 'col'), may hold values from -0.078125 to 0.078125
- tile_rows: int32 [16, 8, 384], P('row', 'col'), may hold values from 0 to 63
- tile_cols: int32 [16, 8, 384], P('row', 'col'), may hold values from 0 to 127
- tile_counts: int32 [16, 8], P('row', 'col'), may hold values from 96 to 384, as said below
- out_grad: bfloat16 [131072, 256], P(('row', 'col')), may hold values from -6 to 6
- features: bfloat16 [131072, 256], P(('row', 'col')), may hold values from -6 to 6
- weight: bfloat16 [256, 256], replicated, may hold values from -0.375 to 0.375
Outputs:
- feat_grad: bfloat16 [131072, 256], P(('row', 'col'))
- weight_grad: float32 [256, 256], replicated
Inputs may be any that keep to these rules, and one draw needn't show every extreme that they name: `tile_counts`: at least one device uses all 384 slots in every draw.
All inputs are finite; a program needn't handle non-finite values.
Results may differ from a plain program's by a relative error of at most 0.015.
Values may be sent and summed in bfloat16 or wider, within the bound.
A program may use at most 256 MiB of HBM per device.

v0:
```python
import jax
import jax.numpy as jnp
from jax import lax
from jax.sharding import PartitionSpec as P


def row_reduce(partial_sum):
    return lax.psum_scatter(partial_sum, "row", scatter_dimension=0, tiled=True)


def weight_reduce(term):
    return lax.psum(term, ("row", "col"))


def split_product(feat_low, exact):
    high = exact.astype(jnp.bfloat16)
    rest = (exact - high.astype(jnp.float32)).astype(jnp.bfloat16)
    dims = (((0,), (0,)), ((), ()))
    first = lax.dot_general(feat_low, high, dims, preferred_element_type=jnp.float32)
    second = lax.dot_general(feat_low, rest, dims, preferred_element_type=jnp.float32)
    return first + second


def per_device(tile_values, tile_rows, tile_cols, tile_counts, out_grad, features, weight):
    values = tile_values[0, 0]
    rows_idx = tile_rows[0, 0]
    cols_idx = tile_cols[0, 0]
    count = tile_counts[0, 0]
    slots = values.shape[0]
    tile = values.shape[1]
    slab = out_grad.shape[0]
    hidden = out_grad.shape[1]
    n_row = lax.axis_size("row")
    group = lax.all_gather(out_grad, "col", axis=0, tiled=True)
    row_tiles = group.shape[0] // tile
    col_tiles = n_row * slab // tile
    group_flat = group.reshape(row_tiles, tile * hidden)
    block = min(slots, 128)
    while slots % block != 0:
        block = block - 1
    steps_count = slots // block
    empty = jnp.zeros((col_tiles, tile * hidden), jnp.float32)
    row_iota = jnp.arange(row_tiles, dtype=jnp.int32)
    col_iota = jnp.arange(col_tiles, dtype=jnp.int32)
    lead = (((0,), (0,)), ((), ()))

    def add_block(carry, step_index):
        first = step_index * block
        vals = lax.dynamic_slice_in_dim(values, first, block, 0)
        rsel = lax.dynamic_slice_in_dim(rows_idx, first, block, 0)
        csel = lax.dynamic_slice_in_dim(cols_idx, first, block, 0)
        used = first + jnp.arange(block, dtype=jnp.int32) < count
        pick_rows = (rsel[:, None] == row_iota[None, :]).astype(jnp.bfloat16)
        picked = jnp.dot(pick_rows, group_flat, preferred_element_type=jnp.float32).astype(
            jnp.bfloat16
        )
        picked = picked.reshape(block, tile, hidden)
        prod = jnp.einsum("tab,tah->tbh", vals, picked, preferred_element_type=jnp.float32)
        prod = prod.reshape(block, tile * hidden)
        place = ((csel[:, None] == col_iota[None, :]) & used[:, None]).astype(jnp.bfloat16)
        high = prod.astype(jnp.bfloat16)
        rest = (prod - high.astype(jnp.float32)).astype(jnp.bfloat16)
        added = lax.dot_general(place, high, lead, preferred_element_type=jnp.float32)
        added = added + lax.dot_general(place, rest, lead, preferred_element_type=jnp.float32)
        return (carry + added, None)

    partial_sum, unused = lax.scan(add_block, empty, jnp.arange(steps_count, dtype=jnp.int32))
    partial_sum = partial_sum.reshape(n_row * slab, hidden)
    scale = 1.0 / jnp.sqrt(jnp.float32(slab * n_row * lax.axis_size("col")))
    back = row_reduce(partial_sum)
    term = split_product(features, back)
    weight_grad = weight_reduce(term) * scale
    back_low = back.astype(jnp.bfloat16)
    feat_grad = lax.dot_general(
        back_low, weight, (((1,), (1,)), ((), ())), preferred_element_type=jnp.float32
    ).astype(jnp.bfloat16)
    return (feat_grad, weight_grad)


def solution(mesh):
    placed = (
        P("row", "col", None, None, None),
        P("row", "col", None),
        P("row", "col", None),
        P("row", "col"),
        P(("row", "col"), None),
        P(("row", "col"), None),
        P(),
    )
    return jax.shard_map(
        per_device,
        mesh=mesh,
        in_specs=placed,
        out_specs=(P(("row", "col"), None), P()),
        check_vma=False,
    )
```

profile of v0, /device:TPU:1, one launch (start us, length us, event | category | flops | bytes accessed | tf_op | source)
XLA Modules:
  0.0 629.6 jit_solution(6691328059924406356)
XLA Ops:
  9.4 16.7 %copy.9 = bf16[1,1,384,128,128]{3,4,2,1,0:T(8,128)(2,1)} copy(bf16[1,1,384,128,128]{4,3,2,1,0:T(8,128)(2,1)} %param.9) | data formatting | bytes 25165824 | tf_op args[0]
  26.1 58.4 %all-gather.2.cloned.1.call-done = bf16[8192,256]{1,0:T(8,128)(2,1)} async-done(((bf16[1024,256]{1,0:T(8,128)(2,1)}), bf16[8192,256]{1,0:T(8,128)(2,1)}) %all-gather.2.cloned.1.call-update) | async-done | bytes 4194320 | tf_op jit(solution)/shard_map/all_gather | solution.py:34
  91.9 268.8 %while.11 = (s32[]{:T(128)}, f32[128,32768]{1,0:T(8,128)}, s32[3]{0:T(128)S(1)}, s32[384]{0:T(512)S(1)}, s32[]{:T(128)}, /*index=5*/bf16[384,128,128]{1,2,0:T(8,...) while((s32[]{:T(128)}, f32[128,32768]{1,0:T(8,128)}, ...), condition=%wide.region_1.2_spmd.clone, body=%wide.region_0.1_spmd.clone.sunk | while | flops 3795919104 | bytes 192942176 | solution.py:67
  93.9 7.8 %convolution_convert_fusion.3 = bf16[128,32768]{1,0:T(8,128)(2,1)} fusion(bf16[64,32768]{1,0:T(8,128)(2,1)} %get-tuple-element.184, s32[128]{0:T(128)S(1)} %dynamic_slice.25), kind=kOutput, calls=%fused_computation.4.clone.1 | convolution fusion | flops 541073408 | bytes 12583424 | tf_op jit(solution)/shard_map/while/body/eval_jaxpr/dot_general | solution.py:54
  101.7 9.1 %copy.15 = bf16[16,8,128,256]{3,2,1,0:T(8,128)(2,1)} copy(bf16[16,8,128,256]{3,1,2,0:T(8,128)(2,1)} %bitcast.32) | data formatting | bytes 16777216 | tf_op jit(solution)/shard_map/while
  110.8 12.7 %fusion.44 = f32[128,128,256]{2,1,0:T(8,128)} fusion(bf16[128,128,256]{2,1,0:T(8,128)(2,1)} %bitcast.31, bf16[384,128,128]{1,2,0:T(8,128)(2,1)} %get-tuple-element.182, s32[]{:T(128)S(6)} %select_n.7), kind=kOutput, calls=%fused_computation.9.clone.1 | convolution fusion | flops 1073741824 | bytes 29360132 | tf_op jit(solution)/shard_map/while/body/eval_jaxpr/tab,tah->tbh/dot_general | solution.py:58
  123.5 17.7 %copy.16 = f32[16,8,128,256]{3,1,2,0:T(8,128)} copy(f32[16,8,128,256]{3,2,1,0:T(8,128)} %bitcast.30) | data formatting | bytes 33554432 | tf_op jit(solution)/shard_map/while
  141.2 13.9 %fusion.45 = f32[128,32768]{1,0:T(8,128)} fusion(f32[128,32768]{1,0:T(8,128)} %bitcast.28, s32[128]{0:T(128)S(1)} %dynamic_slice.26, pred[128]{0:T(512)(128)(4,1)S(1)} %add_compare_fusion.2), kind=kOutput, calls=%fused_computation.7.clone.1 | convolution fusion | flops 1077968896 | bytes 33555072 | tf_op jit(solution)/shard_map/while/body/eval_jaxpr/dot_general | solution.py:63
  155.1 23.2 %fusion.46 = f32[128,32768]{1,0:T(8,128)} fusion(f32[128,32768]{1,0:T(8,128)} %fusion.45, f32[128,32768]{1,0:T(8,128)} %get-tuple-element.166, f32[128,32768]{1,0:T(8,128)} %bitcast.29, pred[]{:T(512)S(6)} %compare.3, s32[128]{0:T(128)S(1)} %dynamic_slice.26, pred[128]{0:T(512)(128)(4,1)S(1)} %add_compare_fusion.2), kind=kOutput, calls=%fused_computation.3.clone.1 | convolution fusion | flops 1103134720 | bytes 67109504 | tf_op jit(solution)/shard_map/while/body/eval_jaxpr/dot_general | solution.py:64
  180.4 7.8 %convolution_convert_fusion.3 = bf16[128,32768]{1,0:T(8,128)(2,1)} fusion(bf16[64,32768]{1,0:T(8,128)(2,1)} %get-tuple-element.184, s32[128]{0:T(128)S(1)} %dynamic_slice.25), kind=kOutput, calls=%fused_computation.4.clone.1 | convolution fusion | flops 541073408 | bytes 12583424 | tf_op jit(solution)/shard_map/while/body/eval_jaxpr/dot_general | solution.py:54
  188.1 9.1 %copy.15 = bf16[16,8,128,256]{3,2,1,0:T(8,128)(2,1)} copy(bf16[16,8,128,256]{3,1,2,0:T(8,128)(2,1)} %bitcast.32) | data formatting | bytes 16777216 | tf_op jit(solution)/shard_map/while
  197.2 12.7 %fusion.44 = f32[128,128,256]{2,1,0:T(8,128)} fusion(bf16[128,128,256]{2,1,0:T(8,128)(2,1)} %bitcast.31, bf16[384,128,128]{1,2,0:T(8,128)(2,1)} %get-tuple-element.182, s32[]{:T(128)S(6)} %select_n.7), kind=kOutput, calls=%fused_computation.9.clone.1 | convolution fusion | flops 1073741824 | bytes 29360132 | tf_op jit(solution)/shard_map/while/body/eval_jaxpr/tab,tah->tbh/dot_general | solution.py:58
  209.9 17.7 %copy.16 = f32[16,8,128,256]{3,1,2,0:T(8,128)} copy(f32[16,8,128,256]{3,2,1,0:T(8,128)} %bitcast.30) | data formatting | bytes 33554432 | tf_op jit(solution)/shard_map/while
  227.6 13.9 %fusion.45 = f32[128,32768]{1,0:T(8,128)} fusion(f32[128,32768]{1,0:T(8,128)} %bitcast.28, s32[128]{0:T(128)S(1)} %dynamic_slice.26, pred[128]{0:T(512)(128)(4,1)S(1)} %add_compare_fusion.2), kind=kOutput, calls=%fused_computation.7.clone.1 | convolution fusion | flops 1077968896 | bytes 33555072 | tf_op jit(solution)/shard_map/while/body/eval_jaxpr/dot_general | solution.py:63
  241.5 28.0 %fusion.46 = f32[128,32768]{1,0:T(8,128)} fusion(f32[128,32768]{1,0:T(8,128)} %fusion.45, f32[128,32768]{1,0:T(8,128)} %get-tuple-element.166, f32[128,32768]{1,0:T(8,128)} %bitcast.29, pred[]{:T(512)S(6)} %compare.3, s32[128]{0:T(128)S(1)} %dynamic_slice.26, pred[128]{0:T(512)(128)(4,1)S(1)} %add_compare_fusion.2), kind=kOutput, calls=%fused_computation.3.clone.1 | convolution fusion | flops 1103134720 | bytes 67109504 | tf_op jit(solution)/shard_map/while/body/eval_jaxpr/dot_general | solution.py:64
  271.6 7.8 %convolution_convert_fusion.3 = bf16[128,32768]{1,0:T(8,128)(2,1)} fusion(bf16[64,32768]{1,0:T(8,128)(2,1)} %get-tuple-element.184, s32[128]{0:T(128)S(1)} %dynamic_slice.25), kind=kOutput, calls=%fused_computation.4.clone.1 | convolution fusion | flops 541073408 | bytes 12583424 | tf_op jit(solution)/shard_map/while/body/eval_jaxpr/dot_general | solution.py:54
  279.3 9.1 %copy.15 = bf16[16,8,128,256]{3,2,1,0:T(8,128)(2,1)} copy(bf16[16,8,128,256]{3,1,2,0:T(8,128)(2,1)} %bitcast.32) | data formatting | bytes 16777216 | tf_op jit(solution)/shard_map/while
  288.4 12.7 %fusion.44 = f32[128,128,256]{2,1,0:T(8,128)} fusion(bf16[128,128,256]{2,1,0:T(8,128)(2,1)} %bitcast.31, bf16[384,128,128]{1,2,0:T(8,128)(2,1)} %get-tuple-element.182, s32[]{:T(128)S(6)} %select_n.7), kind=kOutput, calls=%fused_computation.9.clone.1 | convolution fusion | flops 1073741824 | bytes 29360132 | tf_op jit(solution)/shard_map/while/body/eval_jaxpr/tab,tah->tbh/dot_general | solution.py:58
  301.1 17.7 %copy.16 = f32[16,8,128,256]{3,1,2,0:T(8,128)} copy(f32[16,8,128,256]{3,2,1,0:T(8,128)} %bitcast.30) | data formatting | bytes 33554432 | tf_op jit(solution)/shard_map/while
  318.8 13.9 %fusion.45 = f32[128,32768]{1,0:T(8,128)} fusion(f32[128,32768]{1,0:T(8,128)} %bitcast.28, s32[128]{0:T(128)S(1)} %dynamic_slice.26, pred[128]{0:T(512)(128)(4,1)S(1)} %add_compare_fusion.2), kind=kOutput, calls=%fused_computation.7.clone.1 | convolution fusion | flops 1077968896 | bytes 33555072 | tf_op jit(solution)/shard_map/while/body/eval_jaxpr/dot_general | solution.py:63
  332.7 28.0 %fusion.46 = f32[128,32768]{1,0:T(8,128)} fusion(f32[128,32768]{1,0:T(8,128)} %fusion.45, f32[128,32768]{1,0:T(8,128)} %get-tuple-element.166, f32[128,32768]{1,0:T(8,128)} %bitcast.29, pred[]{:T(512)S(6)} %compare.3, s32[128]{0:T(128)S(1)} %dynamic_slice.26, pred[128]{0:T(512)(128)(4,1)S(1)} %add_compare_fusion.2), kind=kOutput, calls=%fused_computation.3.clone.1 | convolution fusion | flops 1103134720 | bytes 67109504 | tf_op jit(solution)/shard_map/while/body/eval_jaxpr/dot_general | solution.py:64
  360.7 18.0 %reshape.28 = f32[16384,256]{1,0:T(8,128)} reshape(f32[128,32768]{1,0:T(8,128)} %get-tuple-element.54) | data formatting | bytes 33554432 | tf_op jit(solution)/shard_map/reshape | solution.py:68
  378.8 95.3 %reduce-scatter.2.cloned.1.call-done = f32[1024,256]{1,0:T(8,128)} async-done(((f32[16384,256]{1,0:T(8,128)}), f32[1024,256]{1,0:T(8,128)}) %reduce-scatter.2.cloned.1.call-update) | async-done | bytes 1048592 | tf_op jit(solution)/shard_map/reduce_scatter | solution.py:8
  480.7 140.5 %all-reduce.2.cloned.1.call-done = f32[256,256]{0,1:T(8,128)} async-done(((f32[256,256]{0,1:T(8,128)}), f32[256,256]{0,1:T(8,128)}) %all-reduce.2.cloned.1.call-update) | async-done | bytes 262160 | tf_op jit(solution)/shard_map/psum | solution.py:12
  (32 shorter events, 22.2 us)
Async XLA Ops:
  7.2 466.9 %copy-start = (bf16[1024,256]{1,0:T(8,128)(2,1)S(1)}, bf16[1024,256]{1,0:T(8,128)(2,1)}, u32[]{:S(2)}) copy-start(bf16[1024,256]{1,0:T(8,128)(2,1)} %param.14) | copy-start | bytes 1572868
  7.2 77.3 %all-gather.2.cloned.1.call-start = ((), (), s32[]{:S(2)}) async-start(), calls=%async_computation.1 | async-start | bytes 4718592 | tf_op jit(solution)/shard_map/all_gather | solution.py:34
  7.9 466.2 %reduce-scatter.2.cloned.1.call-start = ((), (), s32[]{:S(2)}) async-start(), calls=%async_computation.2 | async-start | bytes 17825792 | tf_op jit(solution)/shard_map/reduce_scatter | solution.py:8
  378.7 99.7 %copy-start.1 = (bf16[256,256]{1,0:T(8,128)(2,1)S(1)}, bf16[256,256]{1,0:T(8,128)(2,1)}, u32[]{:S(2)}) copy-start(bf16[256,256]{1,0:T(8,128)(2,1)} %param.15) | copy-start | bytes 393220
  378.7 242.5 %all-reduce.2.cloned.1.call-start = ((), (), s32[]{:S(2)}) async-start(), calls=%async_computation.3 | async-start | bytes 524288 | tf_op jit(solution)/shard_map/psum | solution.py:12
Sparse Core Ops, SparseCore 0:
  10.4 74.0 all-gather.1
  378.8 95.1 reduce-scatter.1
  479.4 141.7 all-reduce.1
where the time goes:
time: 631 us; the launch traced here: 630 us
  waiting for transfers between devices  295 us (47%)
  matrix products  189 us (30%)
  local copies, waits for them, and re-layouts  125 us (20%)
  between operations  13.8 us (2%)
    psum x1, waiting for transfers between devices, weight_reduce(): return lax.psum(term, ('row', 'col'))  141 us
    reduce_scatter x1, waiting for transfers between devices, row_reduce(): return lax.psum_scatter(partial_sum, 'row', scatter_dimension=0, tiled=True)  95.3 us
    while x6, local copies, waits for them, and re-layouts  80.3 us
    dot_general x3, matrix products, add_block(): lax.dot_general(place, rest, lead, preferred_element_type=jnp.float32)  79.1 us
    all_gather x1, waiting for transfers between devices, per_device(): group = lax.all_gather(out_grad, 'col', axis=0, tiled=True)  58.4 us
    dot_general x3, matrix products, add_block(): lax.dot_general(place, high, lead, preferred_element_type=jnp.float32)  41.8 us
    dot_general x3, matrix products, add_block(): jnp.einsum('tab,tah->tbh', vals, picked, preferred_element_type=jnp.float32)  38.1 us
    dot_general x3, matrix products, add_block(): jnp.dot(pick_rows, group_flat, preferred_element_type=jnp.float32)  23.3 us
  transfers between devices with their start and end apart: 3, of which 3 were waited for; matrix products, arithmetic and copies ran while one was open for 3% of the time, Pallas kernels for 0%

commit v1 on v0

v1 whole, which is shorter than its diff:
```python
import functools

import jax
import jax.numpy as jnp
from jax import lax
from jax.experimental import pallas as pl
from jax.experimental.pallas import tpu as pltpu
from jax.sharding import PartitionSpec as P

MESH = pl.DeviceIdType.MESH
F32 = jnp.float32
BF16 = jnp.bfloat16
TILE = 128
NCOL = 8
NROW = 16
SLAB_TILES = 8
NH = 2
UNROLL = 16


def order_slots(rows_idx, cols_idx, count):
    slots = rows_idx.shape[0]
    col_tiles = NROW * SLAB_TILES
    pairs = (slots + col_tiles) // 2
    t = jnp.arange(slots, dtype=jnp.int32)
    c = jnp.arange(col_tiles, dtype=jnp.int32)
    used = t < count
    key = jnp.where(used, cols_idx, col_tiles)
    before = (key[:, None] == key[None, :]) & (t[None, :] < t[:, None])
    rank = jnp.sum(before.astype(jnp.int32), axis=1)
    hot = key[:, None] == c[None, :]
    number = jnp.sum(hot.astype(jnp.int32), axis=0)
    pair_number = (number + 1) // 2
    first = jnp.sum(jnp.where(c[None, :] < c[:, None], pair_number[None, :], 0), axis=1)
    place = 2 * jnp.sum(jnp.where(hot, first[None, :], 0), axis=1) + rank
    place = jnp.where(used, place, -1)
    q = jnp.arange(2 * pairs, dtype=jnp.int32)
    here = place[None, :] == q[:, None]
    vsrc = slots - jnp.sum(jnp.where(here, slots - t[None, :], 0), axis=1)
    rsrc = jnp.sum(jnp.where(here, rows_idx[None, :], 0), axis=1)
    p = jnp.arange(pairs, dtype=jnp.int32)
    starts = jnp.any((first[None, :] == p[:, None]) & (number[None, :] > 0), axis=1)
    keep = 1.0 - starts.astype(F32)
    last = jnp.where(number > 0, first + pair_number - 1, pairs)
    return vsrc.astype(jnp.int32), rsrc.astype(jnp.int32), keep, last.astype(jnp.int32)


def kernel(
    pairs, scale,
    vsrc, rsrc, keep, last, v_hbm, og_hbm, feat_hbm, w_hbm,
    fg_ref, wg_ref,
    v, og, feat, w, gt0, gt1, s, csend, crecv, q, r2, r1, f1, xr, bt, a_send, a_recv, b_buf, c_buf,
    local, ss, rs,
):
    gt = (gt0, gt1)
    wh = gt0.shape[1]
    slots = v_hbm.shape[0]
    row = lax.axis_index("row")
    col = lax.axis_index("col")
    xl, z, core = row // 8, lax.rem(row // 2, 4), lax.rem(row, 2)
    xh, y = col // 4, lax.rem(col, 4)

    def row_of(dx, dz, dc):
        a = 1 - xl if dx else xl
        b = 1 - core if dc else core
        return a * 8 + lax.rem(z + dz, 4) * 2 + b

    def col_of(dx, dy):
        a = 1 - xh if dx else xh
        return a * 4 + lax.rem(y + dy, 4)

    made = []

    def remote(src, dst, dev):
        i = len(made)
        copy = pltpu.make_async_remote_copy(
            src_ref=src, dst_ref=dst, send_sem=ss.at[i], recv_sem=rs.at[i], device_id=dev, device_id_type=MESH
        )
        made.append(copy)
        return copy

    load_og = pltpu.make_async_copy(og_hbm, og, local.at[0])
    load_v = pltpu.make_async_copy(v_hbm, v.at[pl.ds(0, slots)], local.at[1])
    load_f = pltpu.make_async_copy(feat_hbm, feat, local.at[2])
    load_w = pltpu.make_async_copy(w_hbm, w, local.at[3])
    load_og.start()
    barrier = pltpu.get_barrier_semaphore()
    for d in range(1, NCOL):
        pl.semaphore_signal(barrier, inc=1, device_id=(row, lax.rem(col + d, NCOL)), device_id_type=MESH)
    for d in range(1, NROW):
        pl.semaphore_signal(barrier, inc=1, device_id=(lax.rem(row + d, NROW), col), device_id_type=MESH)
    load_v.start()
    load_f.start()
    load_w.start()

    def turn(h):
        for k in range(SLAB_TILES):
            gt[h][col * SLAB_TILES + k] = og[k * TILE:(k + 1) * TILE, h * wh:(h + 1) * wh].T

    def block(h, dx, dy, half=None):
        at = col_of(dx, dy) * SLAB_TILES
        if half is None:
            return gt[h].at[pl.ds(at, SLAB_TILES)]
        return gt[h].at[pl.ds(at + half * (SLAB_TILES // 2), SLAB_TILES // 2)]

    gather = []
    for h in range(NH):
        m = {}
        m["x"] = remote(block(h, 0, 0), block(h, 0, 0), (row, col_of(1, 0)))
        for side in range(2):
            m["yp", side] = remote(block(h, side, 0), block(h, side, 0), (row, col_of(0, 1)))
            m["ym", side] = remote(block(h, side, 0), block(h, side, 0), (row, col_of(0, 3)))
            m["hp", side] = remote(block(h, side, 3, 0), block(h, side, 3, 0), (row, col_of(0, 1)))
            m["hm", side] = remote(block(h, side, 1, 1), block(h, side, 1, 1), (row, col_of(0, 3)))
        gather.append(m)

    def ag_start(h):
        for name in ("x", ("yp", 0), ("ym", 0)):
            gather[h][name].start()

    def ag_a(h):
        gather[h]["x"].wait_recv()
        gather[h]["yp", 1].start()
        gather[h]["ym", 1].start()

    def ag_b(h, side):
        gather[h]["yp", side].wait_recv()
        gather[h]["hp", side].start()
        gather[h]["ym", side].wait_recv()
        gather[h]["hm", side].start()

    def ag_d(h):
        for side in range(2):
            gather[h]["hp", side].wait_recv()
            gather[h]["hm", side].wait_recv()

    def compute(h, low, high, acc):
        def step(i, acc):
            for u in range(UNROLL):
                p = i * UNROLL + u
                g2 = jnp.concatenate([gt[h][rsrc[2 * p]], gt[h][rsrc[2 * p + 1]]], axis=1)
                v2 = jnp.concatenate([v[vsrc[2 * p]], v[vsrc[2 * p + 1]]], axis=0)
                acc = acc * keep[p] + jnp.dot(g2, v2, preferred_element_type=F32)
                s[p] = acc.astype(BF16)
            return acc

        return lax.fori_loop(low // UNROLL, high // UNROLL, step, acc)

    half_tiles = SLAB_TILES // 2
    order = [(1, 2), (0, 2), (1, 1), (1, 3), (0, 1), (0, 3), (1, 0), (0, 0)]
    reduce = []
    for h in range(NH):
        m = {}
        for dx, dz in order:
            m["c", dx, dz] = remote(csend.at[h, dx * 4 + dz], crecv.at[h, dx * 4 + dz], (row_of(0, 0, 1), col))
        for dx in range(2):
            for d, dz in enumerate((1, 3)):
                dev = (row_of(0, dz, 0), col)
                part = pl.ds(d * half_tiles, half_tiles)
                free = pl.ds((1 - d) * half_tiles, half_tiles)
                m["two", dx, d] = remote(q.at[h, dx * 4 + 2, part], r2.at[h, dx, d], dev)
                m["free", dx, d] = remote(q.at[h, dx * 4 + dz, free], r1.at[h, dx, d, free], dev)
                m["sum", dx, d] = remote(q.at[h, dx * 4 + dz, part], r1.at[h, dx, d, part], dev)
        m["x"] = remote(f1.at[h], xr.at[h], (row_of(1, 0, 0), col))
        reduce.append(m)

    def rs_send(h):
        for dx, dz in order:
            at = row_of(dx, dz, 1) * SLAB_TILES
            for k in range(SLAB_TILES):
                csend[h, dx * 4 + dz, k] = s[last[at + k]]
            reduce[h]["c", dx, dz].start()

    def rs_pair(h):
        for dx, dz in order:
            at = row_of(dx, dz, 0) * SLAB_TILES
            i = dx * 4 + dz
            reduce[h]["c", dx, dz].wait_recv()
            for k in range(SLAB_TILES):
                q[h, i, k] = (s[last[at + k]].astype(F32) + crecv[h, i, k].astype(F32)).astype(BF16)
            if dz == 2:
                reduce[h]["two", dx, 0].start()
                reduce[h]["two", dx, 1].start()
            elif dz == 1:
                reduce[h]["free", dx, 0].start()
            elif dz == 3:
                reduce[h]["free", dx, 1].start()

    def rs_relay(h, dx):
        for d, dz in enumerate((1, 3)):
            reduce[h]["two", dx, d].wait_recv()
            part = pl.ds(d * half_tiles, half_tiles)
            i = dx * 4 + dz
            q[h, i, part] = (q[h, i, part].astype(F32) + r2[h, dx, d].astype(F32)).astype(BF16)
            reduce[h]["sum", dx, d].start()

    def rs_landed(h, dx):
        for d in range(2):
            reduce[h]["free", dx, d].wait_recv()
            reduce[h]["sum", dx, d].wait_recv()

    def rs_cross(h):
        rs_landed(h, 1)
        f1[h] = (q[h, 4].astype(F32) + r1[h, 1, 0].astype(F32) + r1[h, 1, 1].astype(F32)).astype(BF16)
        reduce[h]["x"].start()

    def rs_end(h):
        rs_landed(h, 0)
        reduce[h]["x"].wait_recv()
        for k in range(SLAB_TILES):
            total = (
                q[h, 0, k].astype(F32) + r1[h, 0, 0, k].astype(F32) + r1[h, 0, 1, k].astype(F32) + xr[h, k].astype(F32)
            )
            bt[h * wh:(h + 1) * wh, k * TILE:(k + 1) * TILE] = total.astype(BF16)
        term = jnp.dot(bt[h * wh:(h + 1) * wh, :], feat[...], preferred_element_type=F32)
        chunk = a_send.shape[1]
        for k in range(wh // chunk):
            a_send[h * (wh // chunk) + k] = term[k * chunk:(k + 1) * chunk].astype(BF16)

    load_og.wait()
    turn(0)
    s[pairs] = jnp.zeros((wh, TILE), BF16)
    pl.semaphore_wait(barrier, NCOL + NROW - 2)
    ag_start(0)
    for h in range(1, NH):
        turn(h)
    v[slots] = jnp.zeros((TILE, TILE), BF16)
    ag_a(0)
    ag_b(0, 0)
    ag_start(1)
    ag_b(0, 1)
    ag_d(0)
    load_v.wait()
    load_f.wait()
    load_w.wait()
    half = pairs // 2
    acc = compute(0, 0, half, jnp.zeros((wh, TILE), F32))
    ag_a(1)
    ag_b(1, 0)
    compute(0, half, pairs, acc)
    rs_send(0)
    ag_b(1, 1)
    rs_pair(0)
    rs_relay(0, 1)
    rs_relay(0, 0)
    ag_d(1)
    acc = compute(1, 0, half, jnp.zeros((wh, TILE), F32))
    rs_cross(0)
    compute(1, half, pairs, acc)
    rs_send(1)
    rs_pair(1)
    rs_end(0)
    rs_relay(1, 1)
    rs_relay(1, 0)
    rs_cross(1)
    rs_end(1)

    stage_a = []
    for d in range(1, NCOL):
        to = lax.rem(col + d, NCOL)
        stage_a.append(remote(a_send.at[to], a_recv.at[d - 1], (row, to)))
        stage_a[-1].start()
    stage_b = []
    for d in range(1, NROW):
        stage_b.append(remote(b_buf.at[row], b_buf.at[row], (lax.rem(row + d, NROW), col)))
    stage_c = []
    for d in range(1, NCOL):
        stage_c.append(remote(c_buf.at[col], c_buf.at[col], (row, lax.rem(col + d, NCOL))))

    for k in range(SLAB_TILES):
        fg_ref[k * TILE:(k + 1) * TILE, :] = lax.dot_general(
            bt[:, k * TILE:(k + 1) * TILE], w[...], (((0,), (1,)), ((), ())), preferred_element_type=F32
        ).astype(BF16)

    total = a_send[col].astype(F32)
    for d in range(NCOL - 1):
        stage_a[d].wait_recv()
        total = total + a_recv[d].astype(F32)
    b_buf[row] = total.astype(BF16)
    for copy in stage_b:
        copy.start()
    for copy in stage_b:
        copy.wait_recv()
    total = b_buf[0].astype(F32)
    for i in range(1, NROW):
        total = total + b_buf[i].astype(F32)
    c_buf[col] = total * scale
    for copy in stage_c:
        copy.start()
    for copy in stage_c:
        copy.wait_recv()
    whole = jnp.concatenate([c_buf[i] for i in range(NCOL)], axis=0)
    wg_ref[...] = whole.T
    for copy in made:
        copy.wait_send()


def per_device(tile_values, tile_rows, tile_cols, tile_counts, out_grad, features, weight):
    values = tile_values[0, 0]
    slots = values.shape[0]
    slab, hidden = out_grad.shape
    width = features.shape[1]
    pairs = (slots + NROW * SLAB_TILES) // 2
    wh = hidden // NH
    scale = float(1.0 / (slab * NROW * NCOL) ** 0.5)
    vsrc, rsrc, keep, last = order_slots(tile_rows[0, 0], tile_cols[0, 0], tile_counts[0, 0])
    copies = NH * (9 + 8 + 12 + 1) + 2 * (NCOL - 1) + NROW - 1
    smem = pl.BlockSpec(memory_space=pltpu.SMEM)
    anyspace = pl.BlockSpec(memory_space=pl.ANY)
    vmem = pl.BlockSpec(memory_space=pltpu.VMEM)
    tiles = (SLAB_TILES, wh, TILE)
    half = (SLAB_TILES // 2, wh, TILE)
    return pl.pallas_call(
        functools.partial(kernel, pairs, scale),
        out_shape=(
            jax.ShapeDtypeStruct((slab, width), BF16),
            jax.ShapeDtypeStruct((width, hidden), F32),
        ),
        in_specs=[smem] * 4 + [anyspace] * 4,
        out_specs=(vmem, vmem),
        scratch_shapes=[
            pltpu.VMEM((slots + 1, TILE, TILE), BF16),
            pltpu.VMEM((slab, hidden), BF16),
            pltpu.VMEM((slab, width), BF16),
            pltpu.VMEM((width, hidden), BF16),
            pltpu.VMEM((NCOL * SLAB_TILES, wh, TILE), BF16),
            pltpu.VMEM((NCOL * SLAB_TILES, wh, TILE), BF16),
            pltpu.VMEM((pairs + 1, wh, TILE), BF16),
            pltpu.VMEM((NH, 8) + tiles, BF16),
            pltpu.VMEM((NH, 8) + tiles, BF16),
            pltpu.VMEM((NH, 8) + tiles, BF16),
            pltpu.VMEM((NH, 2, 2) + half, BF16),
            pltpu.VMEM((NH, 2, 2) + tiles, BF16),
            pltpu.VMEM((NH,) + tiles, BF16),
            pltpu.VMEM((NH,) + tiles, BF16),
            pltpu.VMEM((hidden, slab), BF16),
            pltpu.VMEM((NCOL, hidden // NCOL, width), BF16),
            pltpu.VMEM((NCOL - 1, hidden // NCOL, width), BF16),
            pltpu.VMEM((NROW, hidden // NCOL, width), BF16),
            pltpu.VMEM((NCOL, hidden // NCOL, width), F32),
            pltpu.SemaphoreType.DMA((4,)),
            pltpu.SemaphoreType.DMA((copies,)),
            pltpu.SemaphoreType.DMA((copies,)),
        ],
        compiler_params=pltpu.CompilerParams(
            collective_id=0, has_side_effects=True, vmem_limit_bytes=60 * 2**20
        ),
        cost_estimate=pl.CostEstimate(flops=2 * slots * TILE * TILE * hidden, bytes_accessed=16 * 2**20, transcendentals=0),
    )(vsrc, rsrc, keep, last, values, out_grad, features, weight)


def solution(mesh):
    placed = (
        P("row", "col", None, None, None),
        P("row", "col", None),
        P("row", "col", None),
        P("row", "col"),
        P(("row", "col"), None),
        P(("row", "col"), None),
        P(),
    )
    return jax.shard_map(
        per_device,
        mesh=mesh,
        in_specs=placed,
        out_specs=(P(("row", "col"), None), P()),
        check_vma=False,
    )
```

time: 631 us -> 119 us (0.19)
  waiting for transfers between devices: 295 us -> 0 us
  matrix products: 189 us -> 0 us
  local copies, waits for them, and re-layouts: 125 us -> 3.54 us
  Pallas kernels: 0 us -> 109 us
  between operations: 13.8 us -> 1.31 us
    dot_general x15 -> x0, matrix products: 189 us -> none  [the longest x3 79.1 us: add_block(): lax.dot_general(place, rest, lead, preferred_element_type=jnp.float32)]
    psum x1 -> x0, waiting for transfers between devices: 141 us -> none  [weight_reduce(): return lax.psum(term, ('row', 'col'))]
    pallas_call x0 -> x1, Pallas kernels: none -> 109 us  [per_device(): pl.pallas_call(functools.partial(kernel, pairs, scale), out_shape=(jax.Sh...]
    reduce_scatter x1 -> x0, waiting for transfers between devices: 95.3 us -> none  [row_reduce(): return lax.psum_scatter(partial_sum, 'row', scatter_dimension=0, tiled=True)]
    while x6 -> x0, local copies, waits for them, and re-layouts: 80.3 us -> none
    all_gather x1 -> x0, waiting for transfers between devices: 58.4 us -> none  [per_device(): group = lax.all_gather(out_grad, 'col', axis=0, tiled=True)]
    reshape x2 -> x0, local copies, waits for them, and re-layouts: 25.4 us -> none  [the longest x1 18 us: per_device(): partial_sum = partial_sum.reshape(n_row * slab, hidden)]
    unnamed x6 -> x2, local copies, waits for them, and re-layouts: 17.5 us -> 3.54 us
  transfers between devices with their start and end apart: 3 -> 0, of which waited for: 3 -> 0; matrix products, arithmetic and copies ran while one was open for 3% -> 0% of each run, Pallas kernels for 0% -> 0%
where the time goes in v1:
time: 119 us
  Pallas kernels  109 us (92%)
  other arithmetic  4.72 us (4%)
  local copies, waits for them, and re-layouts  3.54 us (3%)
  between operations  1.31 us (1%)
    pallas_call x1, Pallas kernels, per_device(): pl.pallas_call(functools.partial(kernel, pairs, scale), out_shape=(jax.Sh...  109 us
    unnamed x2, local copies, waits for them, and re-layouts  3.54 us

profile of v1, /device:TPU:1, one launch (start us, length us, event | category | flops | bytes accessed | tf_op | source)
XLA Modules:
  0.0 118.7 jit_solution(17820104492727280813)
XLA Ops:
  1.3 0.7 reduce.1
  2.0 0.7 reduce
  2.7 0.1 convert_reduce_fusion.1
  2.8 0.1 select_reduce_fusion.3
  3.0 0.5 add_select_fusion.1.last
  3.5 0.1 fusion.2
  3.6 0.6 convert_subtract_fusion.keep
  4.2 0.2 select_reduce_fusion.2
  4.4 0.2 convert_reduce_fusion
  4.6 0.8 select_reduce_fusion
  5.4 0.6 broadcast_subtract_fusion.vsrc
  6.0 109.1 %shard_map.86 = (bf16[1024,256]{1,0:T(8,128)(2,1)}, f32[256,256]{1,0:T(8,128)}) custom-call(s32[512]{0:T(512)} %broadcast_subtract_fusion.vsrc, s32[512]{0:T(512)} %get-tuple-element.2.rsrc, f32[256]{0:T(256)} %convert_subtract_fusion.keep, s32[128]{0:T(128)} %add_select_fusion.1.last, bf16[384,128,128]{2,1,0:T(8,128)(2,1)} %bitcast.4, ...), custom_call_target="tpu_custom_call" | custom-call | flops 3221225472 | bytes 16777216 | tf_op jit(solution)/shard_map/pallas_call | solution.py:313
  115.2 1.9 %copy.12 = bf16[1024,256]{1,0:T(8,128)(2,1)} copy(bf16[1024,256]{1,0:T(8,128)(2,1)} %get-tuple-element.8) | data formatting | bytes 1048576
  117.0 1.7 %copy.13 = f32[256,256]{1,0:T(8,128)} copy(f32[256,256]{1,0:T(8,128)} %get-tuple-element.9) | data formatting | bytes 524288
  (4 shorter events, 0.0 us)

commit v2 on v1

v2 whole, which is shorter than its diff:
```python
import functools

import jax
import jax.numpy as jnp
from jax import lax
from jax.experimental import pallas as pl
from jax.experimental.pallas import tpu as pltpu
from jax.sharding import PartitionSpec as P

MESH = pl.DeviceIdType.MESH
F32 = jnp.float32
BF16 = jnp.bfloat16
TILE = 128
NCOL = 8
NROW = 16
SLAB_TILES = 8
NH = 2
UNROLL = 16
SEGMENTS = 4
BATCHES = 2


def turned(line, width):
    return jnp.broadcast_to(line, (width, line.shape[1])).T


def order_slots(rows, cols, count, pairs):
    slots = rows.shape[1]
    col_tiles = NROW * SLAB_TILES
    iota = lambda shape, axis: lax.broadcasted_iota(jnp.int32, shape, axis)
    pick = lambda mask, value, axis: jnp.sum(jnp.where(mask, value, 0), axis=axis, keepdims=True)
    t = iota((1, slots), 1)
    key = jnp.where(t < count, cols, col_tiles)
    t_down = iota((slots, TILE), 0)
    key_down = turned(key, TILE)
    rows_down = turned(rows, TILE)
    rank = jnp.zeros((slots, 1), jnp.int32)
    for k in range(0, slots, TILE):
        before = (key_down == key[:, k:k + TILE]) & (t[:, k:k + TILE] < t_down)
        rank = rank + pick(before, 1, 1)
    c = iota((1, col_tiles), 1)
    hot = key_down == c
    number = pick(hot, 1, 0)
    pair_number = (number + 1) >> 1
    lower = iota((col_tiles, col_tiles), 0) < c
    first = pick(lower, turned(pair_number, col_tiles), 0)
    place = 2 * pick(hot, first, 1) + rank
    place = jnp.where(t_down[:, :1] < count, place, -1)
    vsrc, rsrc = [], []
    for k in range(0, 2 * pairs, TILE):
        here = place == iota((1, TILE), 1) + k
        vsrc.append(slots - pick(here, slots - t_down, 0))
        rsrc.append(pick(here, rows_down, 0))
    first_down = turned(first, TILE)
    number_down = turned(number, TILE)
    keep = []
    for k in range(0, pairs, TILE):
        starts = (first_down == iota((1, TILE), 1) + k) & (number_down > 0)
        keep.append((1 - pick(starts, 1, 0)).astype(F32))
    last = jnp.where(number > 0, first + pair_number - 1, pairs)
    return vsrc, rsrc, keep, last


def kernel(
    pairs, scale,
    rows_ref, cols_ref, count_ref, v_hbm, og_hbm, feat_hbm, w_hbm,
    fg_ref, wg_ref,
    index_vm, keep_vm, index, keep, v, og, feat, w, *rest,
):
    gt = rest[:NH]
    s, csend, crecv, q, rx2, r2, r1, r0, f1, xr, bt, a_send, a_recv, b_buf, c_buf, local, ss, rs = rest[NH:]
    wh = gt[0].shape[1]
    slots = v_hbm.shape[2]
    batch_rows = NH * wh // BATCHES
    chunk = batch_rows // NCOL
    row = lax.axis_index("row")
    col = lax.axis_index("col")
    xl, z, core = row // 8, lax.rem(row // 2, 4), lax.rem(row, 2)
    xh, y = col // 4, lax.rem(col, 4)

    def row_of(dx, dz, dc):
        a = 1 - xl if dx else xl
        b = 1 - core if dc else core
        return a * 8 + lax.rem(z + dz, 4) * 2 + b

    def col_of(dx, dy):
        a = 1 - xh if dx else xh
        return a * 4 + lax.rem(y + dy, 4)

    made = []

    def remote(src, dst, dev):
        i = len(made)
        copy = pltpu.make_async_remote_copy(
            src_ref=src, dst_ref=dst, send_sem=ss.at[i], recv_sem=rs.at[i], device_id=dev, device_id_type=MESH
        )
        made.append(copy)
        return copy

    load_og = pltpu.make_async_copy(og_hbm, og, local.at[0])
    load_v = pltpu.make_async_copy(v_hbm.at[0, 0], v.at[pl.ds(0, slots)], local.at[1])
    load_f = pltpu.make_async_copy(feat_hbm, feat, local.at[2])
    load_w = pltpu.make_async_copy(w_hbm, w, local.at[3])
    load_og.start()
    barrier = pltpu.get_barrier_semaphore()
    for d in range(1, NCOL):
        pl.semaphore_signal(barrier, inc=1, device_id=(row, lax.rem(col + d, NCOL)), device_id_type=MESH)
    for d in range(1, NROW):
        pl.semaphore_signal(barrier, inc=1, device_id=(lax.rem(row + d, NROW), col), device_id_type=MESH)
    load_v.start()
    load_f.start()
    load_w.start()

    to_index = pltpu.make_async_copy(index_vm, index, local.at[4])
    to_keep = pltpu.make_async_copy(keep_vm, keep, local.at[5])

    def prepare():
        vsrc, rsrc, chain, last = order_slots(rows_ref[0], cols_ref[0], count_ref[0, 0], pairs)
        for k, line in enumerate(vsrc):
            index_vm[0:1, k * TILE:(k + 1) * TILE] = line
        for k, line in enumerate(rsrc):
            index_vm[1:2, k * TILE:(k + 1) * TILE] = line
        index_vm[2:3, 0:TILE] = last
        for k, line in enumerate(chain):
            keep_vm[0:1, k * TILE:(k + 1) * TILE] = line
        to_index.start()
        to_keep.start()
        v[slots] = jnp.zeros((TILE, TILE), BF16)
        s[pairs] = jnp.zeros((wh, TILE), BF16)

    def loaded():
        to_index.wait()
        to_keep.wait()
        load_v.wait()

    def turn(h):
        for k in range(SLAB_TILES):
            gt[h][col * SLAB_TILES + k] = og[k * TILE:(k + 1) * TILE, h * wh:(h + 1) * wh].T

    def block(h, dx, dy, half=None):
        at = col_of(dx, dy) * SLAB_TILES
        if half is None:
            return gt[h].at[pl.ds(at, SLAB_TILES)]
        return gt[h].at[pl.ds(at + half * (SLAB_TILES // 2), SLAB_TILES // 2)]

    gather = []
    for h in range(NH):
        m = {}
        yp, ym, xp = (row, col_of(0, 1)), (row, col_of(0, 3)), (row, col_of(1, 0))
        m["x1"] = remote(block(h, 0, 0), block(h, 0, 0), xp)
        m["x2"] = remote(block(h, 0, 2), block(h, 0, 2), xp)
        for side in range(2):
            m["yp", side] = remote(block(h, side, 0), block(h, side, 0), yp)
            m["ym", side] = remote(block(h, side, 0), block(h, side, 0), ym)
        m["hp"] = remote(block(h, 0, 3, 0), block(h, 0, 3, 0), yp)
        m["hm"] = remote(block(h, 0, 1, 1), block(h, 0, 1, 1), ym)
        gather.append(m)

    def ag_own(h):
        for name in (("yp", 0), ("ym", 0), "x1"):
            gather[h][name].start()

    def ag_half(h):
        gather[h]["yp", 0].wait_recv()
        gather[h]["hp"].start()
        gather[h]["ym", 0].wait_recv()
        gather[h]["hm"].start()

    def ag_side(h):
        gather[h]["x1"].wait_recv()
        gather[h]["yp", 1].start()
        gather[h]["ym", 1].start()

    def ag_cross(h):
        gather[h]["hp"].wait_recv()
        gather[h]["hm"].wait_recv()
        gather[h]["x2"].start()

    def ag_all(h):
        for name in (("yp", 1), ("ym", 1), "x2"):
            gather[h][name].wait_recv()

    chain = {}

    def compute(h, part):
        def step(i, acc):
            for u in range(UNROLL):
                p = i * UNROLL + u
                g2 = jnp.concatenate([gt[h][index[1, 2 * p]], gt[h][index[1, 2 * p + 1]]], axis=1)
                v2 = jnp.concatenate([v[index[0, 2 * p]], v[index[0, 2 * p + 1]]], axis=0)
                acc = acc * keep[0, p] + jnp.dot(g2, v2, preferred_element_type=F32)
                s[p] = acc.astype(BF16)
            return acc

        steps = pairs // UNROLL // SEGMENTS
        acc = chain[h] if part else jnp.zeros((wh, TILE), F32)
        chain[h] = lax.fori_loop(part * steps, (part + 1) * steps, step, acc)

    half_tiles = SLAB_TILES // 2
    order = [(1, 2), (1, 1), (1, 3), (0, 1), (0, 3), (0, 2), (1, 0), (0, 0)]
    reduce = []
    for h in range(NH):
        m = {}
        xp = (row_of(1, 0, 0), col)
        for dx, dz in order:
            m["c", dx, dz] = remote(csend.at[h, dx * 4 + dz], crecv.at[h, dx * 4 + dz], (row_of(0, 0, 1), col))
        m["x2"] = remote(q.at[h, 6], rx2.at[h], xp)
        for d, dz in enumerate((1, 3)):
            dev = (row_of(0, dz, 0), col)
            part = pl.ds(d * half_tiles, half_tiles)
            free = pl.ds((1 - d) * half_tiles, half_tiles)
            m["side", d] = remote(q.at[h, 4 + dz], r1.at[h, d], dev)
            m["two", d] = remote(q.at[h, 2, part], r2.at[h, d], dev)
            m["free", d] = remote(q.at[h, dz, free], r0.at[h, d, free], dev)
            m["sum", d] = remote(q.at[h, dz, part], r0.at[h, d, part], dev)
        m["x1"] = remote(f1.at[h], xr.at[h], xp)
        reduce.append(m)

    def rs_core(h):
        for dx, dz in order:
            at = row_of(dx, dz, 1) * SLAB_TILES
            for k in range(SLAB_TILES):
                csend[h, dx * 4 + dz, k] = s[index[2, at + k]]
            reduce[h]["c", dx, dz].start()

    def rs_pair(h):
        for dx, dz in order:
            at = row_of(dx, dz, 0) * SLAB_TILES
            i = dx * 4 + dz
            reduce[h]["c", dx, dz].wait_recv()
            for k in range(SLAB_TILES):
                q[h, i, k] = (s[index[2, at + k]].astype(F32) + crecv[h, i, k].astype(F32)).astype(BF16)
            if (dx, dz) == (1, 2):
                reduce[h]["x2"].start()
            elif dz in (1, 3):
                reduce[h]["side" if dx else "free", dz // 2].start()

    def rs_two(h):
        reduce[h]["x2"].wait_recv()
        for d in range(2):
            part = pl.ds(d * half_tiles, half_tiles)
            q[h, 2, part] = (q[h, 2, part].astype(F32) + rx2[h, part].astype(F32)).astype(BF16)
            reduce[h]["two", d].start()

    def rs_cross(h):
        reduce[h]["side", 0].wait_recv()
        reduce[h]["side", 1].wait_recv()
        f1[h] = (q[h, 4].astype(F32) + r1[h, 0].astype(F32) + r1[h, 1].astype(F32)).astype(BF16)
        reduce[h]["x1"].start()

    def rs_sum(h):
        for d, dz in enumerate((1, 3)):
            reduce[h]["two", d].wait_recv()
            part = pl.ds(d * half_tiles, half_tiles)
            q[h, dz, part] = (q[h, dz, part].astype(F32) + r2[h, d].astype(F32)).astype(BF16)
            reduce[h]["sum", d].start()

    def rs_end(h):
        reduce[h]["x1"].wait_recv()
        for d in range(2):
            reduce[h]["free", d].wait_recv()
            reduce[h]["sum", d].wait_recv()
        for k in range(SLAB_TILES):
            total = q[h, 0, k].astype(F32) + r0[h, 0, k].astype(F32) + r0[h, 1, k].astype(F32) + xr[h, k].astype(F32)
            bt[h * wh:(h + 1) * wh, k * TILE:(k + 1) * TILE] = total.astype(BF16)
        term = jnp.dot(bt[h * wh:(h + 1) * wh, :], feat[...], preferred_element_type=F32)
        for k in range(wh // chunk):
            at = h * (wh // chunk) + k
            a_send[at // NCOL, at % NCOL] = term[k * chunk:(k + 1) * chunk].astype(BF16)

    weight = []
    for b in range(BATCHES):
        first, second, third = [], [], []
        for d in range(1, NCOL):
            to = lax.rem(col + d, NCOL)
            first.append(remote(a_send.at[b, to], a_recv.at[b, d - 1], (row, to)))
            third.append(remote(c_buf.at[b, col], c_buf.at[b, col], (row, to)))
        for d in range(1, NROW):
            second.append(remote(b_buf.at[b, row], b_buf.at[b, row], (lax.rem(row + d, NROW), col)))
        weight.append((first, second, third))

    def wg_col(b):
        for copy in weight[b][0]:
            copy.start()

    def wg_row(b):
        total = a_send[b, col].astype(F32)
        for d in range(NCOL - 1):
            weight[b][0][d].wait_recv()
            total = total + a_recv[b, d].astype(F32)
        b_buf[b, row] = total.astype(BF16)
        for copy in weight[b][1]:
            copy.start()

    def wg_back(b):
        for copy in weight[b][1]:
            copy.wait_recv()
        total = b_buf[b, 0].astype(F32)
        for i in range(1, NROW):
            total = total + b_buf[b, i].astype(F32)
        c_buf[b, col] = total.astype(BF16)
        for copy in weight[b][2]:
            copy.start()

    def wg_end(b):
        for copy in weight[b][2]:
            copy.wait_recv()
        whole = jnp.concatenate([c_buf[b, i].astype(F32) for i in range(NCOL)], axis=0)
        wg_ref[:, b * batch_rows:(b + 1) * batch_rows] = whole.T * scale

    def feature():
        for k in range(SLAB_TILES):
            fg_ref[k * TILE:(k + 1) * TILE, :] = lax.dot_general(
                bt[:, k * TILE:(k + 1) * TILE], w[...], (((0,), (1,)), ((), ())), preferred_element_type=F32
            ).astype(BF16)

    load_og.wait()
    turn(0)
    pl.semaphore_wait(barrier, NCOL + NROW - 2)
    ag_own(0)
    turn(1)
    prepare()
    ag_half(0)
    ag_side(0)
    ag_cross(0)
    ag_own(1)
    ag_all(0)
    loaded()
    compute(0, 0)
    compute(0, 1)
    ag_half(1)
    ag_side(1)
    compute(0, 2)
    compute(0, 3)
    rs_core(0)
    ag_cross(1)
    rs_pair(0)
    ag_all(1)
    compute(1, 0)
    compute(1, 1)
    compute(1, 2)
    rs_two(0)
    rs_cross(0)
    compute(1, 3)
    rs_core(1)
    rs_sum(0)
    rs_pair(1)
    load_f.wait()
    load_w.wait()
    rs_end(0)
    wg_col(0)
    rs_two(1)
    rs_cross(1)
    wg_row(0)
    rs_sum(1)
    wg_back(0)
    rs_end(1)
    wg_col(1)
    feature()
    wg_row(1)
    wg_back(1)
    wg_end(0)
    wg_end(1)
    for copy in made:
        copy.wait_send()


def per_device(tile_values, tile_rows, tile_cols, tile_counts, out_grad, features, weight):
    slots = tile_values.shape[2]
    slab, hidden = out_grad.shape
    width = features.shape[1]
    pairs = (slots + NROW * SLAB_TILES) // 2
    wh = hidden // NH
    chunk = hidden // BATCHES // NCOL
    scale = float(1.0 / (slab * NROW * NCOL) ** 0.5)
    copies = NH * 26 + BATCHES * (2 * (NCOL - 1) + NROW - 1)
    smem = pl.BlockSpec(memory_space=pltpu.SMEM)
    anyspace = pl.BlockSpec(memory_space=pl.ANY)
    vmem = pl.BlockSpec(memory_space=pltpu.VMEM)
    tiles = (SLAB_TILES, wh, TILE)
    half = (SLAB_TILES // 2, wh, TILE)
    return pl.pallas_call(
        functools.partial(kernel, pairs, scale),
        out_shape=(
            jax.ShapeDtypeStruct((slab, width), BF16),
            jax.ShapeDtypeStruct((width, hidden), F32),
        ),
        in_specs=[vmem, vmem, smem] + [anyspace] * 4,
        out_specs=(vmem, vmem),
        scratch_shapes=[
            pltpu.VMEM((8, 2 * pairs), jnp.int32),
            pltpu.VMEM((8, pairs), F32),
            pltpu.SMEM((8, 2 * pairs), jnp.int32),
            pltpu.SMEM((8, pairs), F32),
            pltpu.VMEM((slots + 1, TILE, TILE), BF16),
            pltpu.VMEM((slab, hidden), BF16),
            pltpu.VMEM((slab, width), BF16),
            pltpu.VMEM((width, hidden), BF16),
        ]
        + [pltpu.VMEM((NCOL * SLAB_TILES, wh, TILE), BF16) for _ in range(NH)]
        + [
            pltpu.VMEM((pairs + 1, wh, TILE), BF16),
            pltpu.VMEM((NH, 8) + tiles, BF16),
            pltpu.VMEM((NH, 8) + tiles, BF16),
            pltpu.VMEM((NH, 8) + tiles, BF16),
            pltpu.VMEM((NH,) + tiles, BF16),
            pltpu.VMEM((NH, 2) + half, BF16),
            pltpu.VMEM((NH, 2) + tiles, BF16),
            pltpu.VMEM((NH, 2) + tiles, BF16),
            pltpu.VMEM((NH,) + tiles, BF16),
            pltpu.VMEM((NH,) + tiles, BF16),
            pltpu.VMEM((hidden, slab), BF16),
            pltpu.VMEM((BATCHES, NCOL, chunk, width), BF16),
            pltpu.VMEM((BATCHES, NCOL - 1, chunk, width), BF16),
            pltpu.VMEM((BATCHES, NROW, chunk, width), BF16),
            pltpu.VMEM((BATCHES, NCOL, chunk, width), BF16),
            pltpu.SemaphoreType.DMA((6,)),
            pltpu.SemaphoreType.DMA((copies,)),
            pltpu.SemaphoreType.DMA((copies,)),
        ],
        compiler_params=pltpu.CompilerParams(
            collective_id=0, has_side_effects=True, vmem_limit_bytes=60 * 2**20
        ),
        cost_estimate=pl.CostEstimate(flops=2 * slots * TILE * TILE * hidden, bytes_accessed=16 * 2**20, transcendentals=0),
    )(tile_rows, tile_cols, tile_counts, tile_values, out_grad, features, weight)


def solution(mesh):
    placed = (
        P("row", "col", None, None, None),
        P("row", "col", None),
        P("row", "col", None),
        P("row", "col"),
        P(("row", "col"), None),
        P(("row", "col"), None),
        P(),
    )
    return jax.shard_map(
        per_device,
        mesh=mesh,
        in_specs=placed,
        out_specs=(P(("row", "col"), None), P()),
        check_vma=False,
    )
```

time: 119 us -> 99.6 us (0.84)
  Pallas kernels: 109 us -> 94.6 us
  other arithmetic: 4.72 us -> 0 us
    pallas_call x1, Pallas kernels: 109 us -> 94.6 us  [per_device(): pl.pallas_call(functools.partial(kernel, pairs, scale), out_shape=(jax.Sh...]
    reduce_sum x5 -> x0, other arithmetic: 1.5 us -> none  [the longest x1 0.81 us: order_slots(): rsrc = jnp.sum(jnp.where(here, rows_idx[None, :], 0), axis=1)]
    unnamed x2 -> x0, other arithmetic: 1.4 us -> none
where the time goes in v2:
time: 99.6 us; the launch traced here: 99.4 us
  Pallas kernels  94.6 us (95%)
  local copies, waits for them, and re-layouts  3.54 us (4%)
  between operations  1.29 us (1%)
    pallas_call x1, Pallas kernels, per_device(): pl.pallas_call(functools.partial(kernel, pairs, scale), out_shape=(jax.Sh...  94.6 us
    unnamed x2, local copies, waits for them, and re-layouts  3.54 us

profile of v2, /device:TPU:1, one launch (start us, length us, event | category | flops | bytes accessed | tf_op | source)
XLA Modules:
  0.0 99.4 jit_solution(16859213192739157463)
XLA Ops:
  1.3 94.6 %shard_map.86 = (bf16[1024,256]{1,0:T(8,128)(2,1)}, f32[256,256]{1,0:T(8,128)}) custom-call(s32[1,1,384]{2,1,0:T(1,128)} %rows_ref.1, s32[1,1,384]{2,1,0:T(1,128)} %cols_ref.1, s32[1,1]{1,0:T(1,128)S(6)} %copy.11.count_ref, bf16[1,1,384,128,128]{4,3,2,1,0:T(8,128)(2,1)} %v_hbm.1, bf16[1024,256]{1,0:T(8,128)(2,1)} %og_hbm.1, bf16[1024,256]{1,0:T(8,128)(2,1)} %feat_hbm.1, ...), custom_call_target="tpu_custom_call" | custom-call | flops 3221225472 | bytes 16777216 | tf_op jit(solution)/shard_map/pallas_call | solution.py:382
  95.8 1.9 %copy.12 = bf16[1024,256]{1,0:T(8,128)(2,1)} copy(bf16[1024,256]{1,0:T(8,128)(2,1)} %get-tuple-element.4) | data formatting | bytes 1048576
  97.7 1.7 %copy.13 = f32[256,256]{1,0:T(8,128)} copy(f32[256,256]{1,0:T(8,128)} %get-tuple-element.5) | data formatting | bytes 524288

commit v3 on v2

--- a/solution.py
+++ b/solution.py
@@ -14,8 +14,8 @@
 NCOL = 8
 NROW = 16
 SLAB_TILES = 8
-NH = 2
-UNROLL = 16
+NH = 4
+UNROLL = 32
 SEGMENTS = 4
 BATCHES = 2
 
@@ -222,14 +222,16 @@
             for k in range(SLAB_TILES):
                 csend[h, dx * 4 + dz, k] = s[index[2, at + k]]
             reduce[h]["c", dx, dz].start()
+        for dx, dz in order:
+            at = row_of(dx, dz, 0) * SLAB_TILES
+            for k in range(SLAB_TILES):
+                q[h, dx * 4 + dz, k] = s[index[2, at + k]]
 
     def rs_pair(h):
         for dx, dz in order:
-            at = row_of(dx, dz, 0) * SLAB_TILES
             i = dx * 4 + dz
             reduce[h]["c", dx, dz].wait_recv()
-            for k in range(SLAB_TILES):
-                q[h, i, k] = (s[index[2, at + k]].astype(F32) + crecv[h, i, k].astype(F32)).astype(BF16)
+            q[h, i] = (q[h, i].astype(F32) + crecv[h, i].astype(F32)).astype(BF16)
             if (dx, dz) == (1, 2):
                 reduce[h]["x2"].start()
             elif dz in (1, 3):
@@ -319,45 +321,77 @@
     pl.semaphore_wait(barrier, NCOL + NROW - 2)
     ag_own(0)
     turn(1)
+    ag_own(1)
     prepare()
     ag_half(0)
     ag_side(0)
+    turn(2)
     ag_cross(0)
-    ag_own(1)
+    turn(3)
+    ag_half(1)
+    ag_own(2)
+    loaded()
+    ag_cross(1)
+    ag_side(1)
     ag_all(0)
-    loaded()
     compute(0, 0)
     compute(0, 1)
-    ag_half(1)
-    ag_side(1)
+    ag_half(2)
     compute(0, 2)
+    ag_own(3)
     compute(0, 3)
     rs_core(0)
-    ag_cross(1)
-    rs_pair(0)
     ag_all(1)
+    ag_side(2)
     compute(1, 0)
+    ag_cross(2)
     compute(1, 1)
     compute(1, 2)
+    ag_half(3)
+    ag_side(3)
+    rs_pair(0)
+    compute(1, 3)
+    rs_core(1)
+    ag_all(2)
+    compute(2, 0)
+    ag_cross(3)
+    compute(2, 1)
+    rs_pair(1)
+    compute(2, 2)
+    compute(2, 3)
+    rs_core(2)
     rs_two(0)
     rs_cross(0)
-    compute(1, 3)
-    rs_core(1)
+    ag_all(3)
+    compute(3, 0)
+    rs_pair(2)
+    compute(3, 1)
+    compute(3, 2)
+    compute(3, 3)
+    rs_two(1)
+    rs_core(3)
+    rs_cross(1)
     rs_sum(0)
-    rs_pair(1)
+    rs_two(2)
+    rs_pair(3)
+    rs_cross(2)
+    rs_two(3)
+    rs_cross(3)
+    rs_sum(2)
+    rs_sum(1)
+    rs_sum(3)
     load_f.wait()
     load_w.wait()
+    rs_end(2)
     rs_end(0)
+    rs_end(1)
     wg_col(0)
-    rs_two(1)
-    rs_cross(1)
+    rs_end(3)
+    wg_col(1)
     wg_row(0)
-    rs_sum(1)
+    wg_row(1)
+    feature()
     wg_back(0)
-    rs_end(1)
-    wg_col(1)
-    feature()
-    wg_row(1)
     wg_back(1)
     wg_end(0)
     wg_end(1)

time: 99.6 us -> 87.1 us (0.87)
  Pallas kernels: 94.6 us -> 82 us
    pallas_call x1, Pallas kernels: 94.6 us -> 82 us  [per_device(): pl.pallas_call(functools.partial(kernel, pairs, scale), out_shape=(jax.Sh...]
where the time goes in v3:
time: 87.1 us; the launch traced here: 86.9 us
  Pallas kernels  82 us (94%)
  local copies, waits for them, and re-layouts  3.54 us (4%)
  between operations  1.29 us (1%)
    pallas_call x1, Pallas kernels, per_device(): pl.pallas_call(functools.partial(kernel, pairs, scale), out_shape=(jax.Sh...  82 us
    unnamed x2, local copies, waits for them, and re-layouts  3.54 us

profile of v3, /device:TPU:1, one launch (start us, length us, event | category | flops | bytes accessed | tf_op | source)
XLA Modules:
  0.0 86.9 jit_solution(18020208578787288841)
XLA Ops:
  1.3 82.0 %shard_map.86 = (bf16[1024,256]{1,0:T(8,128)(2,1)}, f32[256,256]{1,0:T(8,128)}) custom-call(s32[1,1,384]{2,1,0:T(1,128)} %rows_ref.1, s32[1,1,384]{2,1,0:T(1,128)} %cols_ref.1, s32[1,1]{1,0:T(1,128)S(6)} %copy.11.count_ref, bf16[1,1,384,128,128]{4,3,2,1,0:T(8,128)(2,1)} %v_hbm.1, bf16[1024,256]{1,0:T(8,128)(2,1)} %og_hbm.1, bf16[1024,256]{1,0:T(8,128)(2,1)} %feat_hbm.1, ...), custom_call_target="tpu_custom_call" | custom-call | flops 3221225472 | bytes 16777216 | tf_op jit(solution)/shard_map/pallas_call | solution.py:416
  83.3 1.9 %copy.12 = bf16[1024,256]{1,0:T(8,128)(2,1)} copy(bf16[1024,256]{1,0:T(8,128)(2,1)} %get-tuple-element.4) | data formatting | bytes 1048576
  85.2 1.7 %copy.13 = f32[256,256]{1,0:T(8,128)} copy(f32[256,256]{1,0:T(8,128)} %get-tuple-element.5) | data formatting | bytes 524288

commit v4 on v3

--- a/solution.py
+++ b/solution.py
@@ -17,7 +17,7 @@
 NH = 4
 UNROLL = 32
 SEGMENTS = 4
-BATCHES = 2
+BATCHES = 1
 
 
 def turned(line, width):
@@ -72,7 +72,7 @@
     wh = gt[0].shape[1]
     slots = v_hbm.shape[2]
     batch_rows = NH * wh // BATCHES
-    chunk = batch_rows // NCOL
+    chunk = batch_rows // NROW
     row = lax.axis_index("row")
     col = lax.axis_index("col")
     xl, z, core = row // 8, lax.rem(row // 2, 4), lax.rem(row, 2)
@@ -265,32 +265,34 @@
         for k in range(SLAB_TILES):
             total = q[h, 0, k].astype(F32) + r0[h, 0, k].astype(F32) + r0[h, 1, k].astype(F32) + xr[h, k].astype(F32)
             bt[h * wh:(h + 1) * wh, k * TILE:(k + 1) * TILE] = total.astype(BF16)
-        term = jnp.dot(bt[h * wh:(h + 1) * wh, :], feat[...], preferred_element_type=F32)
-        for k in range(wh // chunk):
-            at = h * (wh // chunk) + k
-            a_send[at // NCOL, at % NCOL] = term[k * chunk:(k + 1) * chunk].astype(BF16)
-
+
+    before = len(made)
     weight = []
     for b in range(BATCHES):
         first, second, third = [], [], []
+        for d in range(1, NROW):
+            to = lax.rem(row + d, NROW)
+            first.append(remote(a_send.at[b, to], a_recv.at[b, d - 1], (to, col)))
+            third.append(remote(c_buf.at[b, row], c_buf.at[b, row], (to, col)))
         for d in range(1, NCOL):
-            to = lax.rem(col + d, NCOL)
-            first.append(remote(a_send.at[b, to], a_recv.at[b, d - 1], (row, to)))
-            third.append(remote(c_buf.at[b, col], c_buf.at[b, col], (row, to)))
-        for d in range(1, NROW):
-            second.append(remote(b_buf.at[b, row], b_buf.at[b, row], (lax.rem(row + d, NROW), col)))
+            second.append(remote(b_buf.at[b, col], b_buf.at[b, col], (row, lax.rem(col + d, NCOL))))
         weight.append((first, second, third))
+
+    def wg_term(low, high):
+        term = jnp.dot(bt[low:high, :], feat[...], preferred_element_type=F32)
+        for k in range(low // chunk, high // chunk):
+            a_send[k // NROW, k % NROW] = term[k * chunk - low:(k + 1) * chunk - low].astype(BF16)
 
     def wg_col(b):
         for copy in weight[b][0]:
             copy.start()
 
     def wg_row(b):
-        total = a_send[b, col].astype(F32)
-        for d in range(NCOL - 1):
+        total = a_send[b, row].astype(F32)
+        for d in range(NROW - 1):
             weight[b][0][d].wait_recv()
             total = total + a_recv[b, d].astype(F32)
-        b_buf[b, row] = total.astype(BF16)
+        b_buf[b, col] = total.astype(BF16)
         for copy in weight[b][1]:
             copy.start()
 
@@ -298,16 +300,16 @@
         for copy in weight[b][1]:
             copy.wait_recv()
         total = b_buf[b, 0].astype(F32)
-        for i in range(1, NROW):
+        for i in range(1, NCOL):
             total = total + b_buf[b, i].astype(F32)
-        c_buf[b, col] = total.astype(BF16)
+        c_buf[b, row] = total.astype(BF16)
         for copy in weight[b][2]:
             copy.start()
 
     def wg_end(b):
         for copy in weight[b][2]:
             copy.wait_recv()
-        whole = jnp.concatenate([c_buf[b, i].astype(F32) for i in range(NCOL)], axis=0)
+        whole = jnp.concatenate([c_buf[b, i].astype(F32) for i in range(NROW)], axis=0)
         wg_ref[:, b * batch_rows:(b + 1) * batch_rows] = whole.T * scale
 
     def feature():
@@ -321,81 +323,81 @@
     pl.semaphore_wait(barrier, NCOL + NROW - 2)
     ag_own(0)
     turn(1)
+    prepare()
     ag_own(1)
-    prepare()
     ag_half(0)
     ag_side(0)
+    ag_half(1)
+    loaded()
+    ag_cross(0)
     turn(2)
-    ag_cross(0)
-    turn(3)
-    ag_half(1)
     ag_own(2)
-    loaded()
+    ag_side(1)
     ag_cross(1)
-    ag_side(1)
     ag_all(0)
     compute(0, 0)
     compute(0, 1)
+    turn(3)
     ag_half(2)
     compute(0, 2)
     ag_own(3)
     compute(0, 3)
+    ag_side(2)
     rs_core(0)
+    ag_cross(2)
     ag_all(1)
-    ag_side(2)
     compute(1, 0)
-    ag_cross(2)
     compute(1, 1)
+    rs_pair(0)
+    ag_half(3)
     compute(1, 2)
-    ag_half(3)
+    compute(1, 3)
     ag_side(3)
-    rs_pair(0)
-    compute(1, 3)
     rs_core(1)
     ag_all(2)
     compute(2, 0)
     ag_cross(3)
     compute(2, 1)
+    rs_two(0)
+    compute(2, 2)
     rs_pair(1)
-    compute(2, 2)
     compute(2, 3)
     rs_core(2)
-    rs_two(0)
-    rs_cross(0)
+    rs_sum(0)
     ag_all(3)
     compute(3, 0)
+    compute(3, 1)
     rs_pair(2)
-    compute(3, 1)
     compute(3, 2)
+    rs_two(1)
     compute(3, 3)
-    rs_two(1)
+    rs_cross(0)
     rs_core(3)
-    rs_cross(1)
-    rs_sum(0)
-    rs_two(2)
     rs_pair(3)
     rs_cross(2)
+    rs_two(2)
+    rs_cross(1)
     rs_two(3)
+    rs_end(0)
+    rs_sum(1)
     rs_cross(3)
     rs_sum(2)
-    rs_sum(1)
     rs_sum(3)
+    rs_end(2)
+    rs_end(1)
     load_f.wait()
     load_w.wait()
-    rs_end(2)
-    rs_end(0)
-    rs_end(1)
+    wg_term(0, (NH - 1) * wh)
+    rs_end(3)
+    wg_term((NH - 1) * wh, NH * wh)
     wg_col(0)
-    rs_end(3)
-    wg_col(1)
+    feature()
+    for copy in made[:before]:
+        copy.wait_send()
     wg_row(0)
-    wg_row(1)
-    feature()
     wg_back(0)
-    wg_back(1)
     wg_end(0)
-    wg_end(1)
-    for copy in made:
+    for copy in made[before:]:
         copy.wait_send()
 
 
@@ -405,9 +407,9 @@
     width = features.shape[1]
     pairs = (slots + NROW * SLAB_TILES) // 2
     wh = hidden // NH
-    chunk = hidden // BATCHES // NCOL
+    chunk = hidden // BATCHES // NROW
     scale = float(1.0 / (slab * NROW * NCOL) ** 0.5)
-    copies = NH * 26 + BATCHES * (2 * (NCOL - 1) + NROW - 1)
+    copies = NH * 26 + BATCHES * (2 * (NROW - 1) + NCOL - 1)
     smem = pl.BlockSpec(memory_space=pltpu.SMEM)
     anyspace = pl.BlockSpec(memory_space=pl.ANY)
     vmem = pl.BlockSpec(memory_space=pltpu.VMEM)
@@ -444,10 +446,10 @@
             pltpu.VMEM((NH,) + tiles, BF16),
             pltpu.VMEM((NH,) + tiles, BF16),
             pltpu.VMEM((hidden, slab), BF16),
+            pltpu.VMEM((BATCHES, NROW, chunk, width), BF16),
+            pltpu.VMEM((BATCHES, NROW - 1, chunk, width), BF16),
             pltpu.VMEM((BATCHES, NCOL, chunk, width), BF16),
-            pltpu.VMEM((BATCHES, NCOL - 1, chunk, width), BF16),
             pltpu.VMEM((BATCHES, NROW, chunk, width), BF16),
-            pltpu.VMEM((BATCHES, NCOL, chunk, width), BF16),
             pltpu.SemaphoreType.DMA((6,)),
             pltpu.SemaphoreType.DMA((copies,)),
             pltpu.SemaphoreType.DMA((copies,)),

time: 87.1 us -> 85.2 us (0.978)
  Pallas kernels: 82 us -> 80.2 us
    pallas_call x1, Pallas kernels: 82 us -> 80.2 us  [per_device(): pl.pallas_call(functools.partial(kernel, pairs, scale), out_shape=(jax.Sh...]
where the time goes in v4:
time: 85.2 us; the launch traced here: 85 us
  Pallas kernels  80.2 us (94%)
  local copies, waits for them, and re-layouts  3.54 us (4%)
  between operations  1.29 us (2%)
    pallas_call x1, Pallas kernels, per_device(): pl.pallas_call(functools.partial(kernel, pairs, scale), out_shape=(jax.Sh...  80.2 us
    unnamed x2, local copies, waits for them, and re-layouts  3.54 us

profile of v4, /device:TPU:1, one launch (start us, length us, event | category | flops | bytes accessed | tf_op | source)
XLA Modules:
  0.0 85.0 jit_solution(8703904239475691696)
XLA Ops:
  1.3 80.2 %shard_map.86 = (bf16[1024,256]{1,0:T(8,128)(2,1)}, f32[256,256]{1,0:T(8,128)}) custom-call(s32[1,1,384]{2,1,0:T(1,128)} %rows_ref.1, s32[1,1,384]{2,1,0:T(1,128)} %cols_ref.1, s32[1,1]{1,0:T(1,128)S(6)} %copy.11.count_ref, bf16[1,1,384,128,128]{4,3,2,1,0:T(8,128)(2,1)} %v_hbm.1, bf16[1024,256]{1,0:T(8,128)(2,1)} %og_hbm.1, bf16[1024,256]{1,0:T(8,128)(2,1)} %feat_hbm.1, ...), custom_call_target="tpu_custom_call" | custom-call | flops 3221225472 | bytes 16777216 | tf_op jit(solution)/shard_map/pallas_call | solution.py:418
  81.5 1.9 %copy.12 = bf16[1024,256]{1,0:T(8,128)(2,1)} copy(bf16[1024,256]{1,0:T(8,128)(2,1)} %get-tuple-element.4) | data formatting | bytes 1048576
  83.3 1.7 %copy.13 = f32[256,256]{1,0:T(8,128)} copy(f32[256,256]{1,0:T(8,128)} %get-tuple-element.5) | data formatting | bytes 524288

commit v5 on v4

--- a/solution.py
+++ b/solution.py
@@ -270,12 +270,14 @@
     weight = []
     for b in range(BATCHES):
         first, second, third = [], [], []
-        for d in range(1, NROW):
-            to = lax.rem(row + d, NROW)
-            first.append(remote(a_send.at[b, to], a_recv.at[b, d - 1], (to, col)))
+        for k, (dx, dz, dc) in enumerate(
+            (dx, dz, dc) for dx in (1, 0) for dz in (2, 1, 3, 0) for dc in (1, 0) if dx or dz or dc
+        ):
+            to = row_of(dx, dz, dc)
+            first.append(remote(a_send.at[b, to], a_recv.at[b, k], (to, col)))
             third.append(remote(c_buf.at[b, row], c_buf.at[b, row], (to, col)))
-        for d in range(1, NCOL):
-            second.append(remote(b_buf.at[b, col], b_buf.at[b, col], (row, lax.rem(col + d, NCOL))))
+        for dx, dy in ((1, 2), (1, 1), (1, 3), (1, 0), (0, 2), (0, 1), (0, 3)):
+            second.append(remote(b_buf.at[b, col], b_buf.at[b, col], (row, col_of(dx, dy))))
         weight.append((first, second, third))
 
     def wg_term(low, high):

time: 85.2 us -> 85.1 us (level)
  no operation moved by 1% of the time
where the time goes in v5:
time: 85.1 us; the launch traced here: 84.8 us
  Pallas kernels  80 us (94%)
  local copies, waits for them, and re-layouts  3.54 us (4%)
  between operations  1.29 us (2%)
    pallas_call x1, Pallas kernels, per_device(): pl.pallas_call(functools.partial(kernel, pairs, scale), out_shape=(jax.Sh...  80 us
    unnamed x2, local copies, waits for them, and re-layouts  3.54 us

profile of v5, /device:TPU:1, one launch (start us, length us, event | category | flops | bytes accessed | tf_op | source)
XLA Modules:
  0.0 84.8 jit_solution(12866704442029080969)
XLA Ops:
  1.3 80.0 %shard_map.86 = (bf16[1024,256]{1,0:T(8,128)(2,1)}, f32[256,256]{1,0:T(8,128)}) custom-call(s32[1,1,384]{2,1,0:T(1,128)} %rows_ref.1, s32[1,1,384]{2,1,0:T(1,128)} %cols_ref.1, s32[1,1]{1,0:T(1,128)S(6)} %copy.11.count_ref, bf16[1,1,384,128,128]{4,3,2,1,0:T(8,128)(2,1)} %v_hbm.1, bf16[1024,256]{1,0:T(8,128)(2,1)} %og_hbm.1, bf16[1024,256]{1,0:T(8,128)(2,1)} %feat_hbm.1, ...), custom_call_target="tpu_custom_call" | custom-call | flops 3221225472 | bytes 16777216 | tf_op jit(solution)/shard_map/pallas_call | solution.py:420
  81.3 1.9 %copy.12 = bf16[1024,256]{1,0:T(8,128)(2,1)} copy(bf16[1024,256]{1,0:T(8,128)(2,1)} %get-tuple-element.4) | data formatting | bytes 1048576
  83.2 1.7 %copy.13 = f32[256,256]{1,0:T(8,128)} copy(f32[256,256]{1,0:T(8,128)} %get-tuple-element.5) | data formatting | bytes 524288
